TPU v7x, 512 devices: a whole 4x8x8 slice. The times are simulated.
512 devices in a mesh: blk: 32 (over z, y_lo), uly: 16 (over x, y_hi, core).
Axes of the slice: x: 4, y: 8 (y_hi: 2, y_lo: 4; y = y_hi * 4 + y_lo), z: 8, core: 2. Of those that a mesh axis runs over, the one named last changes fastest.
Arguments:
- span_q: bfloat16 [1024, 4096], P(('blk', 'uly')), may hold values from -9 to 9
- span_k: bfloat16 [1024, 4096], P(('blk', 'uly')), may hold values from -9 to 9
- span_v: bfloat16 [1024, 4096], P(('blk', 'uly')), may hold values from -6 to 6
- span_grad: bfloat16 [1024, 4096], P(('blk', 'uly')), may hold values from -6 to 6
- mem_k: bfloat16 [31744, 4096], P(('blk', 'uly')), may hold values from -6 to 6
- mem_v: bfloat16 [31744, 4096], P(('blk', 'uly')), may hold values from -6 to 6
- retrieved: int32 [2, 32], replicated, may hold values from 0 to 61, all different within a row
- tile_keep: int32 [2, 248], replicated, may hold values 0 or 1
Outputs:
- grad_q: float32 [1024, 4096], P(('blk', 'uly'))
- grad_k: float32 [1024, 4096], P(('blk', 'uly'))
- grad_v: float32 [1024, 4096], P(('blk', 'uly'))
- grad_mem_k: float32 [31744, 4096], P(('blk', 'uly'))
- grad_mem_v: float32 [31744, 4096], P(('blk', 'uly'))
Inputs may be any that keep to these rules, and one draw needn't show every extreme that they name: `retrieved`: each row names 32 different past frames, and every past frame is named by some row.
All inputs are finite; a program needn't handle non-finite values.
Results may differ from a plain program's by a relative error of at most 0.0047.
Values may be sent and summed in bfloat16 or wider, within the bound.
No kernel may reach another device: no remote copies, remote signals or barrier semaphores. Data moves between devices by JAX's collectives and lax.ppermute only.
A program may use at most 64 MiB of HBM per device.

v0:
```python
import math

import jax
import jax.numpy as jnp
from jax import lax
from jax.sharding import PartitionSpec as P

DH = 128
QF = 2
MF = 62
FT = 4


masked_score = -1e30


def local(span_q, span_k, span_v, span_grad, mem_k, mem_v, retrieved, tile_keep):
    regrouped = (
        lax.all_to_all(span_q, "uly", split_axis=1, concat_axis=0, tiled=True),
        lax.all_to_all(span_k, "uly", split_axis=1, concat_axis=0, tiled=True),
        lax.all_to_all(span_v, "uly", split_axis=1, concat_axis=0, tiled=True),
        lax.all_to_all(span_grad, "uly", split_axis=1, concat_axis=0, tiled=True),
        lax.all_to_all(mem_k, "uly", split_axis=1, concat_axis=0, tiled=True),
        lax.all_to_all(mem_v, "uly", split_axis=1, concat_axis=0, tiled=True),
    )
    queries, span_keys, span_values, out_grads, memory_keys, memory_values = regrouped
    row_count = queries.shape[0]
    memory_rows = memory_keys.shape[0]
    feat_width = queries.shape[1]
    head_count = feat_width // DH
    cycle_size = lax.axis_size("blk")
    cycle_rank = lax.axis_index("blk")
    span_rows = row_count * cycle_size
    frame_len = span_rows // QF
    tile_len = frame_len // FT
    score_scale = 1.0 / math.sqrt(DH)
    key_rows = memory_rows + row_count
    block_len = math.gcd(key_rows, 256)
    block_count = key_rows // block_len
    key_blocks = jnp.concatenate([memory_keys, span_keys], axis=0).reshape(
        block_count, block_len, head_count, DH
    )
    value_blocks = jnp.concatenate([memory_values, span_values], axis=0).reshape(
        block_count, block_len, head_count, DH
    )
    memory_pos = cycle_rank * memory_rows + jnp.arange(memory_rows, dtype=jnp.int32)
    span_pos = cycle_rank * row_count + jnp.arange(row_count, dtype=jnp.int32)
    frame_ids = jnp.arange(MF, dtype=jnp.int32)
    chosen = jnp.any(retrieved[:, :, None] == frame_ids[None, None, :], axis=1).astype(jnp.float32)
    frame_onehot = (memory_pos[:, None] // frame_len == frame_ids[None, :]).astype(jnp.float32)
    tile_ids = jnp.arange(MF * FT, dtype=jnp.int32)
    tile_onehot = (memory_pos[:, None] // tile_len == tile_ids[None, :]).astype(jnp.float32)
    memory_table = jnp.dot(chosen, frame_onehot.T) * jnp.dot(
        tile_keep.astype(jnp.float32), tile_onehot.T
    )
    query_frame_ids = jnp.arange(QF, dtype=jnp.int32)
    span_table = (span_pos[None, :] // frame_len <= query_frame_ids[:, None]).astype(jnp.float32)
    key_table = jnp.concatenate([memory_table, span_table], axis=1)
    key_table = key_table.reshape(QF, block_count, block_len).transpose(1, 0, 2)

    def block_scores(query_three, frame_pick, key_piece, table_piece):
        permit = jnp.dot(frame_pick, table_piece) > 0.5
        raw_scores = (
            jnp.einsum("qhd,khd->hqk", query_three, key_piece, preferred_element_type=jnp.float32)
            * score_scale
        )
        return (permit, jnp.where(permit[None], raw_scores, masked_score))

    all_queries, all_grads = (
        lax.all_gather(queries, "blk", axis=0, tiled=True),
        lax.all_gather(out_grads, "blk", axis=0, tiled=True),
    )
    query_three = all_queries.reshape(span_rows, head_count, DH)
    grad_three = all_grads.reshape(span_rows, head_count, DH)
    query_frame = jnp.arange(span_rows, dtype=jnp.int32) // frame_len
    frame_pick = (query_frame[:, None] == query_frame_ids[None, :]).astype(jnp.float32)

    def stats_visit(carry, block_items):
        run_max, run_sum, run_dot = carry
        key_piece, value_piece, table_piece = block_items
        permit, scores = block_scores(query_three, frame_pick, key_piece, table_piece)
        new_max = jnp.maximum(run_max, jnp.max(scores, axis=2))
        weights = jnp.where(permit[None], jnp.exp(scores - new_max[:, :, None]), 0.0)
        rescale = jnp.exp(run_max - new_max)
        products = jnp.einsum(
            "qhd,khd->hqk", grad_three, value_piece, preferred_element_type=jnp.float32
        )
        run_sum = run_sum * rescale + jnp.sum(weights, axis=2)
        run_dot = run_dot * rescale + jnp.sum(weights * products, axis=2)
        return ((new_max, run_sum, run_dot), None)

    stats_init = (
        jnp.full((head_count, span_rows), masked_score, jnp.float32),
        jnp.zeros((head_count, span_rows), jnp.float32),
        jnp.zeros((head_count, span_rows), jnp.float32),
    )
    (run_max, run_sum, run_dot), _ = lax.scan(
        stats_visit, stats_init, (key_blocks, value_blocks, key_table)
    )
    glob_max = lax.pmax(run_max, "blk")
    rescale = jnp.exp(run_max - glob_max)
    glob_sum, glob_dot = lax.psum((run_sum * rescale, run_dot * rescale), "blk")
    log_total = glob_max + jnp.log(glob_sum)
    row_delta = glob_dot / glob_sum

    def score_grads(
        query_part,
        grad_part,
        pick_part,
        total_part,
        delta_part,
        key_piece,
        value_piece,
        table_piece,
    ):
        permit, scores = block_scores(query_part, pick_part, key_piece, table_piece)
        probs = jnp.where(permit[None], jnp.exp(scores - total_part[:, :, None]), 0.0)
        products = jnp.einsum(
            "qhd,khd->hqk", grad_part, value_piece, preferred_element_type=jnp.float32
        )
        dscore = (probs * (products - delta_part[:, :, None])).astype(jnp.bfloat16)
        return (probs, dscore)

    def key_side(probs, dscore):
        value_grad = jnp.einsum(
            "hqk,qhd->khd",
            probs.astype(jnp.bfloat16),
            grad_three,
            preferred_element_type=jnp.float32,
        )
        key_grad = (
            jnp.einsum("hqk,qhd->khd", dscore, query_three, preferred_element_type=jnp.float32)
            * score_scale
        )
        return (key_grad, value_grad)

    def grad_visit(query_acc, block_items):
        key_piece, value_piece, table_piece = block_items
        probs, dscore = score_grads(
            query_three,
            grad_three,
            frame_pick,
            log_total,
            row_delta,
            key_piece,
            value_piece,
            table_piece,
        )
        term = (
            jnp.einsum("hqk,khd->qhd", dscore, key_piece, preferred_element_type=jnp.float32)
            * score_scale
        )
        return (query_acc + term, key_side(probs, dscore))

    query_acc, (key_grad, value_grad) = lax.scan(
        grad_visit,
        jnp.zeros((span_rows, head_count, DH), jnp.float32),
        (key_blocks, value_blocks, key_table),
    )
    query_grad = lax.psum_scatter(
        query_acc.reshape(span_rows, feat_width), "blk", scatter_dimension=0, tiled=True
    )
    key_grad = key_grad.reshape(key_rows, feat_width)
    value_grad = value_grad.reshape(key_rows, feat_width)
    restored = (
        lax.all_to_all(query_grad, "uly", split_axis=0, concat_axis=1, tiled=True),
        lax.all_to_all(key_grad[memory_rows:], "uly", split_axis=0, concat_axis=1, tiled=True),
        lax.all_to_all(value_grad[memory_rows:], "uly", split_axis=0, concat_axis=1, tiled=True),
        lax.all_to_all(key_grad[:memory_rows], "uly", split_axis=0, concat_axis=1, tiled=True),
        lax.all_to_all(value_grad[:memory_rows], "uly", split_axis=0, concat_axis=1, tiled=True),
    )
    return (restored[0], restored[1], restored[2], restored[3], restored[4])


def solution(mesh):
    return jax.shard_map(
        local,
        mesh=mesh,
        in_specs=(
            P(("blk", "uly"), None),
            P(("blk", "uly"), None),
            P(("blk", "uly"), None),
            P(("blk", "uly"), None),
            P(("blk", "uly"), None),
            P(("blk", "uly"), None),
            P(),
            P(),
        ),
        out_specs=(
            P(("blk", "uly"), None),
            P(("blk", "uly"), None),
            P(("blk", "uly"), None),
            P(("blk", "uly"), None),
            P(("blk", "uly"), None),
        ),
        check_vma=False,
    )
```

profile of v0, /device:TPU:1, one launch (start us, length us, event | category | flops | bytes accessed | tf_op | source)
XLA Modules:
  0.0 766.8 jit_solution(9719503115892516533)
XLA Ops:
  7.2 20.8 %all_to_all.209 = bf16[2,16,256]{2,0,1:T(2,128)(2,1)S(1)} all-to-all(bf16[2,16,256]{2,0,1:T(2,128)(2,1)} %bitcast.206), channel_id=1, replica_groups=mesh['blk'=32,'uly'=16] {'uly'}, dimensions={1} | all-to-all | bytes 32768 | tf_op jit(solution)/shard_map/all_to_all | solution.py:19
  27.9 13.4 %all_to_all.210 = bf16[2,16,256]{2,0,1:T(2,128)(2,1)S(1)} all-to-all(bf16[2,16,256]{2,0,1:T(2,128)(2,1)} %bitcast.207), channel_id=1, replica_groups=mesh['blk'=32,'uly'=16] {'uly'}, dimensions={1} | all-to-all | bytes 32768 | tf_op jit(solution)/shard_map/all_to_all | solution.py:20
  41.3 13.4 %all_to_all.211 = bf16[2,16,256]{2,0,1:T(2,128)(2,1)S(1)} all-to-all(bf16[2,16,256]{2,0,1:T(2,128)(2,1)} %bitcast.208), channel_id=1, replica_groups=mesh['blk'=32,'uly'=16] {'uly'}, dimensions={1} | all-to-all | bytes 32768 | tf_op jit(solution)/shard_map/all_to_all | solution.py:21
  54.8 3.7 all-to-all-start.5
  58.4 1.2 copy.92
  59.7 0.9 copy.64
  60.6 7.5 all-to-all-done.5
  68.2 3.8 all-to-all-start
  72.2 1.0 copy.69
  73.9 13.8 %all-to-all-done = bf16[62,16,256]{2,0,1:T(8,128)(2,1)S(1)} async-done(((bf16[62,16,256]{2,0,1:T(8,128)(2,1)}), bf16[62,16,256]{2,0,1:T(8,128)(2,1)S(1)}, u32[]{:S(2)}, u32[]{:S(2)}) %all-to-all-start) | async-done | bytes 507936 | tf_op jit(solution)/shard_map/all_to_all | solution.py:23
  87.8 4.4 all-to-all-start.3
  92.3 82.7 %all_gather.7 = bf16[1024,256]{1,0:T(8,128)(2,1)S(1)} all-gather(bf16[32,256]{1,0:T(8,128)(2,1)S(1)} %all_to_all.177), channel_id=1, replica_groups=mesh['blk'=32,'uly'=16] {'blk'}, dimensions={0}, use_global_device_ids=true | all-gather | bytes 540672 | tf_op jit(solution)/shard_map/all_gather | solution.py:71
  175.6 63.6 %all_gather.6 = bf16[1024,256]{1,0:T(8,128)(2,1)S(1)} all-gather(bf16[32,256]{1,0:T(8,128)(2,1)S(1)} %all_to_all.165), channel_id=1, replica_groups=mesh['blk'=32,'uly'=16] {'blk'}, dimensions={0}, use_global_device_ids=true | all-gather | bytes 540672 | tf_op jit(solution)/shard_map/all_gather | solution.py:70
  239.2 1.0 copy.68
  240.2 1.3 copy.78
  241.5 0.9 all_to_all.157
  242.4 1.1 pad_maximum_fusion
  243.5 0.9 reshape.189
  244.4 1.1 copy.77
  245.5 0.9 all_to_all.169
  246.5 1.1 pad_maximum_fusion.1
  247.5 0.9 reshape.192
  248.4 1.1 copy.75
  249.6 10.6 %while.30 = (s32[]{:T(128)}, f32[2,1024]{1,0:T(2,128)S(1)}, f32[2,1024]{1,0:T(2,128)S(1)}, f32[2,1024]{1,0:T(2,128)S(1)}, bf16[4,2,256]{2,1,0:T(2,128)(2,1)S(1)}...) while((s32[]{:T(128)}, f32[2,1024]{1,0:T(2,128)S(1)}, ...), condition=%wide.region_5.6_spmd.clone, body=%wide.region_1.5_spmd.clone.sunk | while | flops 277104640 | bytes 8803476 | solution.py:97
  250.7 0.9 fusion.108
  253.4 0.9 fusion.108
  256.0 0.9 fusion.108
  258.7 0.9 fusion.108
  260.2 63.4 %pmax.7 = f32[2,1024]{1,0:T(2,128)S(1)} all-reduce(f32[2,1024]{1,0:T(2,128)S(1)} %get-tuple-element.123), channel_id=1, replica_groups=mesh['blk'=32,'uly'=16] {'blk'}, use_global_device_ids=true, to_apply=%region_6.7 | all-reduce | flops 2048 | bytes 16384 | tf_op jit(solution)/shard_map/pmax | solution.py:100
  323.7 121.0 %all-reduce = (f32[2,1024]{1,0:T(2,128)S(1)}, f32[2,1024]{1,0:T(2,128)S(1)}) all-reduce(f32[2,1024]{1,0:T(2,128)S(1)} %get-tuple-element.326, f32[2,1024]{1,0:T(2,128)S(1)} %get-tuple-element.325), channel_id=1, replica_groups=mesh['blk'=32,'uly'=16] {'blk'}, use_global_device_ids=true, to_apply=%region_7.8 | all-reduce | flops 4096 | bytes 32768 | tf_op jit(solution)/shard_map/psum | solution.py:102
  444.6 17.4 %while.31 = (s32[]{:T(128)}, f32[1024,2,128]{0,2,1:T(8,128)S(1)}, f32[4,256,2,128]{3,2,1,0:T(2,128)}, f32[4,256,2,128]{3,2,1,0:T(2,128)}, bf16[4,256,2,128]{3,1,...) while((s32[]{:T(128)}, f32[1024,2,128]{0,2,1:T(8,128)S(1)}, ...), condition=%wide.region_10.11_spmd.clone, body=%wide.region_9.10_spmd.clone.sunk | while | flops 677449728 | bytes 16143531 | solution.py:155
  445.2 0.8 fusion.124
  447.8 1.2 copy_dynamic-update-slice_fusion.3
  449.5 0.8 fusion.124
  452.1 1.2 copy_dynamic-update-slice_fusion.3
  453.9 0.8 fusion.124
  456.5 1.2 copy_dynamic-update-slice_fusion.3
  458.2 0.8 fusion.124
  460.8 1.2 copy_dynamic-update-slice_fusion.3
  462.0 1.3 copy.102
  463.3 0.6 all_to_all.186
  464.0 76.3 %all-to-all-start.8 = ((f32[16,2,256]{2,1,0:T(2,128)}), f32[16,2,256]{2,1,0:T(2,128)S(1)}, u32[]{:S(2)}, u32[]{:S(2)}) async-start(f32[16,2,256]{2,1,0:T(2,128)} %all_to_all.186), calls=%async_computation.9 | async-start | bytes 65536 | tf_op jit(solution)/shard_map/all_to_all | solution.py:168
  540.3 1.3 copy.103
  541.6 0.6 all_to_all.182
  542.2 7.8 %all-to-all-done.8 = f32[16,2,256]{2,1,0:T(2,128)S(1)} async-done(((f32[16,2,256]{2,1,0:T(2,128)}), f32[16,2,256]{2,1,0:T(2,128)S(1)}, u32[]{:S(2)}, u32[]{:S(2)}) %all-to-all-start.8) | async-done | bytes 32800 | tf_op jit(solution)/shard_map/all_to_all | solution.py:168
  550.0 3.7 all-to-all-start.7
  553.7 1.0 slice.19
  554.7 2.3 all_to_all.194
  557.0 6.4 all-to-all-done.7
  563.4 4.0 all-to-all-start.10
  567.5 1.3 copy.81
  568.9 1.1 all_to_all.190
  570.0 24.7 %all-to-all-done.10 = f32[16,62,256]{2,1,0:T(8,128)S(1)} async-done(((f32[16,62,256]{2,1,0:T(8,128)}), f32[16,62,256]{2,1,0:T(8,128)S(1)}, u32[]{:S(2)}, u32[]{:S(2)}) %all-to-all-start.10) | async-done | bytes 1015840 | tf_op jit(solution)/shard_map/all_to_all | solution.py:170
  594.7 7.4 all-to-all-start.9
  602.1 112.2 %reduce-scatter.2.cloned.1.call-done = f32[32,256]{1,0:T(8,128)} async-done(((f32[1024,256]{1,0:T(8,128)}), f32[32,256]{1,0:T(8,128)}) %reduce-scatter.2.cloned.1.call-update) | async-done | bytes 32784 | tf_op jit(solution)/shard_map/reduce_scatter | solution.py:160
  714.3 1.4 all_to_all.178
  715.7 32.8 %all-to-all-start.6 = ((f32[16,2,256]{2,1,0:T(2,128)}), f32[16,2,256]{2,1,0:T(2,128)S(1)}, u32[]{:S(2)}, u32[]{:S(2)}) async-start(f32[16,2,256]{2,1,0:T(2,128)} %all_to_all.178), calls=%async_computation.7 | async-start | bytes 65536 | tf_op jit(solution)/shard_map/all_to_all | solution.py:166
  748.4 0.6 copy.85
  749.1 1.6 copy.97
  751.3 1.6 copy.96
  752.9 5.2 all-to-all-done.6
  758.1 0.6 copy.135
  758.8 0.6 copy.136
  759.4 0.6 copy.137
  (85 shorter events, 18.6 us)
Async XLA Ops:
  54.8 13.4 %all-to-all-start.5 = ((bf16[2,16,256]{2,0,1:T(2,128)(2,1)}), bf16[2,16,256]{2,0,1:T(2,128)(2,1)S(1)}, u32[]{:S(2)}, u32[]{:S(2)}) async-start(bf16[2,16,256]{2,0,1:T(2,128)(2,1)} %bitcast.209), calls=%async_computation.5 | async-start | bytes 32768 | tf_op jit(solution)/shard_map/all_to_all | solution.py:22
  58.4 13.6 %copy-start = (bf16[62,4096]{1,0:T(8,128)(2,1)S(1)}, bf16[62,4096]{1,0:T(8,128)(2,1)}, u32[]{:S(2)}) copy-start(bf16[62,4096]{1,0:T(8,128)(2,1)} %param.17) | copy-start | bytes 1523716
  60.6 12.5 %copy-start.2 = (s32[2,32]{1,0:T(2,128)S(1)}, s32[2,32]{1,0:T(2,128)}, u32[]{:S(2)}) copy-start(s32[2,32]{1,0:T(2,128)} %param.18) | copy-start | bytes 772
  60.6 12.9 %copy-start.1 = (s32[2,248]{1,0:T(2,128)S(1)}, s32[2,248]{1,0:T(2,128)}, u32[]{:S(2)}) copy-start(s32[2,248]{1,0:T(2,128)} %param.19) | copy-start | bytes 5956
  68.2 19.6 %all-to-all-start = ((bf16[62,16,256]{2,0,1:T(8,128)(2,1)}), bf16[62,16,256]{2,0,1:T(8,128)(2,1)S(1)}, u32[]{:S(2)}, u32[]{:S(2)}) async-start(bf16[62,16,256]{2,0,1:T(8,128)(2,1)} %copy.64), calls=%async_computation | async-start | bytes 1048576 | tf_op jit(solution)/shard_map/all_to_all | solution.py:23
  87.8 157.8 %all-to-all-start.3 = ((bf16[62,16,256]{2,0,1:T(8,128)(2,1)}), bf16[62,16,256]{2,0,1:T(8,128)(2,1)S(1)}, u32[]{:S(2)}, u32[]{:S(2)}) async-start(bf16[62,16,256]{2,0,1:T(8,128)(2,1)} %copy.69), calls=%async_computation.3 | async-start | bytes 1048576 | tf_op jit(solution)/shard_map/all_to_all | solution.py:24
  464.0 86.0 %all-to-all-start.8 = ((f32[16,2,256]{2,1,0:T(2,128)}), f32[16,2,256]{2,1,0:T(2,128)S(1)}, u32[]{:S(2)}, u32[]{:S(2)}) async-start(f32[16,2,256]{2,1,0:T(2,128)} %all_to_all.186), calls=%async_computation.9 | async-start | bytes 65536 | tf_op jit(solution)/shard_map/all_to_all | solution.py:168
  550.0 13.4 %all-to-all-start.7 = ((f32[16,2,256]{2,1,0:T(2,128)}), f32[16,2,256]{2,1,0:T(2,128)S(1)}, u32[]{:S(2)}, u32[]{:S(2)}) async-start(f32[16,2,256]{2,1,0:T(2,128)} %all_to_all.182), calls=%async_computation.8 | async-start | bytes 65536 | tf_op jit(solution)/shard_map/all_to_all | solution.py:167
  563.4 31.2 %all-to-all-start.10 = ((f32[16,62,256]{2,1,0:T(8,128)}), f32[16,62,256]{2,1,0:T(8,128)S(1)}, u32[]{:S(2)}, u32[]{:S(2)}) async-start(f32[16,62,256]{2,1,0:T(8,128)} %all_to_all.194), calls=%async_computation.11 | async-start | bytes 2097152 | tf_op jit(solution)/shard_map/all_to_all | solution.py:170
  567.5 146.8 %reduce-scatter.2.cloned.1.call-start = ((), (), s32[]{:S(2)}) async-start(), calls=%async_computation.12 | async-start | bytes 1081344 | tf_op jit(solution)/shard_map/reduce_scatter | solution.py:160
  594.7 121.0 %all-to-all-start.9 = ((f32[16,62,256]{2,1,0:T(8,128)}), f32[16,62,256]{2,1,0:T(8,128)S(1)}, u32[]{:S(2)}, u32[]{:S(2)}) async-start(f32[16,62,256]{2,1,0:T(8,128)} %all_to_all.190), calls=%async_computation.10 | async-start | bytes 2097152 | tf_op jit(solution)/shard_map/all_to_all | solution.py:169
  715.7 42.5 %all-to-all-start.6 = ((f32[16,2,256]{2,1,0:T(2,128)}), f32[16,2,256]{2,1,0:T(2,128)S(1)}, u32[]{:S(2)}, u32[]{:S(2)}) async-start(f32[16,2,256]{2,1,0:T(2,128)} %all_to_all.178), calls=%async_computation.7 | async-start | bytes 65536 | tf_op jit(solution)/shard_map/all_to_all | solution.py:166
Sparse Core Ops, SparseCore 0:
  571.7 142.5 reduce-scatter.1
where the time goes:
time: 768 us; the launch traced here: 767 us
  blocking collectives  378 us (49%)
  waiting for transfers between devices  178 us (23%)
  starting transfers between devices  136 us (18%)
  local copies, waits for them, and re-layouts  34.2 us (4%)
  matrix products  21 us (3%)
  between operations  14.3 us (2%)
    psum x1, blocking collectives, local(): glob_sum, glob_dot = lax.psum((run_sum * rescale, run_dot * rescale), 'blk')  121 us
    reduce_scatter x1, waiting for transfers between devices, local(): lax.psum_scatter(query_acc.reshape(span_rows, feat_width), 'blk', scatter...  112 us
    all_gather x1, blocking collectives, local(): lax.all_gather(out_grads, 'blk', axis=0, tiled=True)  82.7 us
    all_to_all x1, starting transfers between devices, local(): lax.all_to_all(value_grad[memory_rows:], 'uly', split_axis=0, concat_axis...  76.3 us
    all_gather x1, blocking collectives, local(): lax.all_gather(queries, 'blk', axis=0, tiled=True)  63.6 us
    pmax x1, blocking collectives, local(): glob_max = lax.pmax(run_max, 'blk')  63.4 us
    all_to_all x1, starting transfers between devices, local(): lax.all_to_all(query_grad, 'uly', split_axis=0, concat_axis=1, tiled=True)  32.8 us
    all_to_all x1, waiting for transfers between devices, local(): lax.all_to_all(value_grad[:memory_rows], 'uly', split_axis=0, concat_axis...  24.7 us
  transfers between devices with their start and end apart: 9, of which 7 were waited for; matrix products, arithmetic and copies ran while one was open for 2% of the time, Pallas kernels for 0%

commit v1 on v0

v1 whole, which is shorter than its diff:
```python
import math

import jax
import jax.numpy as jnp
from jax import lax
from jax.experimental import pallas as pl
from jax.experimental.pallas import tpu as pltpu
from jax.sharding import Mesh, PartitionSpec as P

DH = 128
HEADS = 32
QF = 2
MF = 62
FT = 4
FRAME = 512
TILE = 128
MEM_ROWS = 62
SPAN_ROWS = 2
ROWS = MEM_ROWS + SPAN_ROWS

FINE = (("zh", 4), ("zl", 2), ("ym", 2), ("yl", 2), ("x", 4), ("yh", 2), ("core", 2))
NAMES = tuple(name for name, _ in FINE)
SIZES = tuple(size for _, size in FINE)
HEAD_AXES = ("zl", "yl", "x", "core")
KEY_AXES = ("zh", "ym", "yh")
GROUPS = 16

HALF = FRAME // HEADS
CHUNK = 512
SOURCES = CHUNK // ROWS
K_AT, V_AT, Q_AT, G_AT = 0, ROWS, 2 * ROWS, 2 * ROWS + 2 * HALF
SENT = 2 * ROWS + 4 * HALF
BACK = 2 * ROWS + 2 * HALF
WIDE = HEADS * DH // 2
LOG2E = math.log2(math.e)
SCALE = 1.0 / math.sqrt(DH)
BARRED = -1e30
FLOOR = -1e20


def load_queries(in_ref, qt_ref, gt_ref):
    pick = lax.broadcasted_iota(jnp.int32, (DH, FRAME), 0)
    for f in range(QF):
        q = in_ref[:, Q_AT + f * HALF : Q_AT + (f + 1) * HALF, :].reshape(FRAME, DH)
        g = in_ref[:, G_AT + f * HALF : G_AT + (f + 1) * HALF, :].reshape(FRAME, DH)
        qt_ref[f, 0:DH, :] = q.T
        qt_ref[f, DH : 2 * DH, :] = jnp.where(pick == f, 1.0, 0.0).astype(jnp.bfloat16)
        gt_ref[f] = g.T


def load_keys(in_ref, mask_ref, c):
    sources = pl.ds(c * SOURCES, SOURCES)
    keys = in_ref[sources, K_AT : K_AT + ROWS, :].reshape(CHUNK, DH)
    values = in_ref[sources, V_AT : V_AT + ROWS, :].reshape(CHUNK, DH)
    start = pl.multiple_of(c * CHUNK, CHUNK)
    masked_keys = jnp.concatenate([keys, mask_ref[pl.ds(start, CHUNK), :]], axis=1)
    return keys, masked_keys, values


def dot(a, b):
    return jnp.dot(a, b, preferred_element_type=jnp.float32)


def stats_kernel(in_ref, mask_ref, out_ref, qt_ref, gt_ref, max_ref, sum_ref, dot_ref):
    load_queries(in_ref, qt_ref, gt_ref)
    max_ref[...] = jnp.full(max_ref.shape, FLOOR, jnp.float32)
    sum_ref[...] = jnp.zeros(sum_ref.shape, jnp.float32)
    dot_ref[...] = jnp.zeros(dot_ref.shape, jnp.float32)

    def visit(c, carry):
        _, masked_keys, values = load_keys(in_ref, mask_ref, c)
        for f in range(QF):
            scores = (dot(masked_keys, qt_ref[f]) * (SCALE * LOG2E)).reshape(CHUNK // 8, 8, FRAME)
            products = dot(values, gt_ref[f]).reshape(CHUNK // 8, 8, FRAME)
            old = max_ref[f]
            new = jnp.maximum(old, jnp.max(scores, axis=0))
            weights = jnp.exp2(scores - new[None])
            rescale = jnp.exp2(old - new)
            max_ref[f] = new
            sum_ref[f] = sum_ref[f] * rescale + jnp.sum(weights, axis=0)
            dot_ref[f] = dot_ref[f] * rescale + jnp.sum(weights * products, axis=0)
        return carry

    lax.fori_loop(0, HEADS * ROWS // CHUNK, visit, 0)
    logs, means = [], []
    for f in range(QF):
        top = jnp.max(max_ref[f], axis=0, keepdims=True)
        rescale = jnp.exp2(max_ref[f] - top)
        total = jnp.sum(sum_ref[f] * rescale, axis=0, keepdims=True)
        inner = jnp.sum(dot_ref[f] * rescale, axis=0, keepdims=True)
        some = total > 0.0
        safe = jnp.where(some, total, 1.0)
        log_row = jnp.where(some, top + jnp.log(safe) * LOG2E, BARRED)
        mean_row = inner / safe
        logs += [log_row[:, :256], log_row[:, 256:]]
        means += [mean_row[:, :256], mean_row[:, 256:]]
    stats = jnp.concatenate(logs + means, axis=0)
    out_ref[...] = jnp.broadcast_to(stats[None], out_ref.shape)


def grads_kernel(in_ref, mask_ref, stats_ref, out_ref, qt_ref, gt_ref, acc_ref):
    load_queries(in_ref, qt_ref, gt_ref)
    acc_ref[...] = jnp.zeros(acc_ref.shape, jnp.float32)
    logs = stats_ref[:, 0:4, :]
    means = stats_ref[:, 4:8, :]
    top = jnp.max(logs, axis=0)
    weights = jnp.exp2(logs - top[None])
    total = jnp.sum(weights, axis=0)
    log_total = top + jnp.log(total) * LOG2E
    delta = jnp.sum(weights * means, axis=0) / total

    def row(stat, f):
        return jnp.concatenate([stat[2 * f : 2 * f + 1], stat[2 * f + 1 : 2 * f + 2]], axis=1)

    log_rows = [row(log_total, f) for f in range(QF)]
    delta_rows = [row(delta, f) for f in range(QF)]

    def visit(c, carry):
        keys, masked_keys, values = load_keys(in_ref, mask_ref, c)
        keys_t = keys.T
        key_grad = jnp.zeros((CHUNK, DH), jnp.float32)
        value_grad = jnp.zeros((CHUNK, DH), jnp.float32)
        for f in range(QF):
            q = in_ref[:, Q_AT + f * HALF : Q_AT + (f + 1) * HALF, :].reshape(FRAME, DH)
            g = in_ref[:, G_AT + f * HALF : G_AT + (f + 1) * HALF, :].reshape(FRAME, DH)
            scores = dot(masked_keys, qt_ref[f]) * (SCALE * LOG2E)
            probs = jnp.exp2(scores - log_rows[f])
            products = dot(values, gt_ref[f])
            dscore = (probs * (products - delta_rows[f])).astype(jnp.bfloat16)
            value_grad += dot(probs.astype(jnp.bfloat16), g)
            key_grad += dot(dscore, q)
            acc_ref[f] += dot(keys_t, dscore)
        sources = pl.ds(c * SOURCES, SOURCES)
        out_ref[sources, K_AT : K_AT + ROWS, :] = (
            (key_grad * SCALE).astype(jnp.bfloat16).reshape(SOURCES, ROWS, DH)
        )
        out_ref[sources, V_AT : V_AT + ROWS, :] = value_grad.astype(jnp.bfloat16).reshape(
            SOURCES, ROWS, DH
        )
        return carry

    lax.fori_loop(0, HEADS * ROWS // CHUNK, visit, 0)
    for f in range(QF):
        query_grad = (acc_ref[f].T * SCALE).astype(jnp.bfloat16)
        out_ref[:, Q_AT + f * HALF : Q_AT + (f + 1) * HALF, :] = query_grad.reshape(HEADS, HALF, DH)


def mask_rows(retrieved, tile_keep):
    tiles = jnp.arange(256, dtype=jnp.int32)
    chosen = jnp.any(retrieved[:, :, None] == (tiles // FT)[None, None, :], axis=1)
    kept = jnp.pad(tile_keep, ((0, 0), (0, 256 - MF * FT))) == 1
    own = (tiles[None, :] >= MF * FT) & (
        tiles[None, :] - MF * FT <= jnp.arange(QF, dtype=jnp.int32)[:, None]
    )
    barred = 1.0 - ((chosen & kept) | own).astype(jnp.float32)
    barred = jnp.pad(barred, ((0, DH - QF), (0, 0)))
    row = jnp.arange(HEADS * ROWS, dtype=jnp.int32)
    source, inner = row // ROWS, row % ROWS
    place = {"core": source % 2, "x": source // 2 % 4, "yl": source // 8 % 2, "zl": source // 16}
    device = 0
    for name, size in FINE:
        device = device * size + (place[name] if name in place else lax.axis_index(name))
    tile = jnp.where(
        inner < MEM_ROWS,
        (device * MEM_ROWS + inner) // TILE,
        MF * FT + (device * SPAN_ROWS + inner - MEM_ROWS) // FRAME,
    )
    onehot = (tile[:, None] == tiles[None, :]).astype(jnp.float32)
    hit = lax.dot_general(onehot, barred, (((1,), (1,)), ((), ())))
    return jnp.where(hit > 0.5, BARRED, 0.0).astype(jnp.bfloat16)


def spread_kernel(q_ref, g_ref, out_ref):
    rows = jnp.concatenate(
        [part[:, half] for part in (q_ref, g_ref) for half in (slice(0, WIDE), slice(WIDE, 2 * WIDE))],
        axis=0,
    )
    for b in range(0, GROUPS, 2):
        out_ref[8 * b : 8 * (b + 2), :] = jnp.concatenate([rows, rows], axis=0)


def moved(order, rows):
    count = rows.shape[0]
    to = lax.broadcasted_iota(jnp.int32, (count, count), 0)
    at = lax.broadcasted_iota(jnp.int32, (count, count), 1)
    pick = jnp.where(order(to) == at, 1.0, 0.0).astype(jnp.bfloat16)
    return dot(pick, rows).astype(jnp.bfloat16)


def pack_kernel(gathered_ref, mem_k_ref, span_k_ref, mem_v_ref, span_v_ref, out_ref):
    rows = moved(
        lambda i: (i // 2 % 16) * 8 + (i // 32 % 2) * 4 + (i // 64) * 2 + i % 2, gathered_ref[...]
    )
    for h in range(HEADS):
        lanes = slice(h * DH, (h + 1) * DH)
        out_ref[h, K_AT : K_AT + MEM_ROWS, :] = mem_k_ref[:, lanes]
        out_ref[h, K_AT + MEM_ROWS : K_AT + ROWS, :] = span_k_ref[:, lanes]
        out_ref[h, V_AT : V_AT + MEM_ROWS, :] = mem_v_ref[:, lanes]
        out_ref[h, V_AT + MEM_ROWS : V_AT + ROWS, :] = span_v_ref[:, lanes]
        half, at = divmod(h * DH, WIDE)
        out_ref[h, Q_AT:SENT, :] = rows[half * 4 * HALF : (half + 1) * 4 * HALF, at : at + DH]


def unpack_queries_kernel(back_ref, out_ref):
    quarters = []
    for quarter in range(4):
        heads = [back_ref[quarter * 8 + i, Q_AT:BACK, :] for i in range(8)]
        quarters.append(jnp.concatenate(heads, axis=1))
    rows = jnp.concatenate(quarters, axis=0)
    out_ref[...] = moved(lambda i: (i // 2 % 4) * 32 + (i // 8) * 2 + i % 2, rows)


def unpack_keys_kernel(back_ref, mem_k_ref, mem_v_ref, span_k_ref, span_v_ref):
    for h in range(HEADS):
        lanes = slice(h * DH, (h + 1) * DH)
        key_grad = back_ref[h, K_AT : K_AT + ROWS, :].astype(jnp.float32)
        value_grad = back_ref[h, V_AT : V_AT + ROWS, :].astype(jnp.float32)
        mem_k_ref[:, lanes] = key_grad[:MEM_ROWS]
        mem_v_ref[:, lanes] = value_grad[:MEM_ROWS]
        span_k_ref[:, lanes] = key_grad[MEM_ROWS:]
        span_v_ref[:, lanes] = value_grad[MEM_ROWS:]


def call(kernel, name, out_shape, scratch_shapes=(), flops=0, transcendentals=0, moved_bytes=2 << 20):
    return pl.pallas_call(
        kernel,
        out_shape=out_shape,
        scratch_shapes=list(scratch_shapes),
        compiler_params=pltpu.CompilerParams(vmem_limit_bytes=40 * 1024 * 1024),
        cost_estimate=pl.CostEstimate(
            flops=flops, bytes_accessed=moved_bytes, transcendentals=transcendentals
        ),
        name=name,
    )


def shape(dims, dtype):
    return jax.ShapeDtypeStruct(dims, dtype)


def local(span_q, span_k, span_v, span_grad, mem_k, mem_v, retrieved, tile_keep):
    bf16, f32 = jnp.bfloat16, jnp.float32
    pairs = HEADS * ROWS * QF * FRAME
    queries = [pltpu.VMEM((QF, 2 * DH, FRAME), bf16), pltpu.VMEM((QF, DH, FRAME), bf16)]
    sums = [pltpu.VMEM((QF, 8, FRAME), f32)] * 3

    spread = call(spread_kernel, "spread", shape((8 * GROUPS, WIDE), bf16))(span_q, span_grad)
    gathered = lax.all_to_all(spread, KEY_AXES, 0, 0, tiled=True)
    packed = call(pack_kernel, "pack", shape((HEADS, SENT, DH), bf16))(
        gathered, mem_k, span_k, mem_v, span_v
    )
    held = lax.all_to_all(packed, HEAD_AXES, 0, 0, tiled=True)

    mask = mask_rows(retrieved, tile_keep)
    stats = call(
        stats_kernel,
        "stats",
        shape((GROUPS, 8, 256), f32),
        queries + sums,
        flops=6 * pairs * DH,
        transcendentals=pairs,
    )(held, mask)
    stats = lax.all_to_all(stats, KEY_AXES, 0, 0, tiled=True)
    grads = call(
        grads_kernel,
        "grads",
        shape((HEADS, BACK, DH), bf16),
        queries + [pltpu.VMEM((QF, DH, FRAME), f32)],
        flops=12 * pairs * DH,
        transcendentals=pairs,
    )(held, mask, stats)

    back = lax.all_to_all(grads, HEAD_AXES, 0, 0, tiled=True)
    parts = call(unpack_queries_kernel, "unpack_queries", shape((8 * GROUPS, WIDE // 2), bf16))(back)
    parts = lax.all_to_all(parts, KEY_AXES, 0, 0, tiled=True)
    grad_mem_k, grad_mem_v, grad_k, grad_v = call(
        unpack_keys_kernel,
        "unpack_keys",
        (shape((MEM_ROWS, HEADS * DH), f32),) * 2 + (shape((SPAN_ROWS, HEADS * DH), f32),) * 2,
        moved_bytes=4 << 20,
    )(back)
    grad_q = jnp.sum(parts.reshape(GROUPS, 4, SPAN_ROWS, WIDE // 2).astype(f32), axis=0)
    grad_q = grad_q.transpose(1, 0, 2).reshape(SPAN_ROWS, HEADS * DH)
    return grad_q, grad_k, grad_v, grad_mem_k, grad_mem_v


def solution(mesh):
    fine = Mesh(mesh.devices.reshape(SIZES), NAMES)
    rows = P(NAMES, None)
    return jax.shard_map(
        local,
        mesh=fine,
        in_specs=(rows,) * 6 + (P(), P()),
        out_specs=(rows,) * 5,
        check_vma=False,
    )
```

time: 768 us -> 140 us (0.18)
  blocking collectives: 378 us -> 76.2 us
  waiting for transfers between devices: 178 us -> 34.3 us
  starting transfers between devices: 136 us -> 11 us
  local copies, waits for them, and re-layouts: 34.2 us -> 2.17 us
  matrix products: 21 us -> 0.76 us
  Pallas kernels: 0 us -> 14.1 us
  between operations: 14.3 us -> 0.79 us
    all_gather x2 -> x0, blocking collectives: 146 us -> none  [the longest x1 82.7 us: local(): lax.all_gather(out_grads, 'blk', axis=0, tiled=True)]
    all_to_all x8 -> x2, starting transfers between devices: 136 us -> 11 us  [the longest x1 7.5 us: local(): held = lax.all_to_all(packed, HEAD_AXES, 0, 0, tiled=True)]
    psum x1 -> x0, blocking collectives: 121 us -> none  [local(): glob_sum, glob_dot = lax.psum((run_sum * rescale, run_dot * rescale), 'blk')]
    reduce_scatter x1 -> x0, waiting for transfers between devices: 112 us -> none  [local(): lax.psum_scatter(query_acc.reshape(span_rows, feat_width), 'blk', scatter...]
    pmax x1 -> x0, blocking collectives: 63.4 us -> none  [local(): glob_max = lax.pmax(run_max, 'blk')]
    all_to_all x8 -> x2, waiting for transfers between devices: 65.5 us -> 34.3 us  [the longest x1 21.9 us: local(): held = lax.all_to_all(packed, HEAD_AXES, 0, 0, tiled=True)]
    all_to_all x3, blocking collectives: 47.6 us -> 76.2 us  [the longest x1 34.9 us: local(): gathered = lax.all_to_all(spread, KEY_AXES, 0, 0, tiled=True)]
    dot_general x38 -> x1, matrix products: 21 us -> 0.76 us  [mask_rows(): hit = lax.dot_general(onehot, barred, (((1,), (1,)), ((), ())))]
  transfers between devices with their start and end apart: 9 -> 2, of which waited for: 7 -> 2; matrix products, arithmetic and copies ran while one was open for 2% -> 1% of each run, Pallas kernels for 0% -> 1%
where the time goes in v1:
time: 140 us
  blocking collectives  76.2 us (54%)
  waiting for transfers between devices  34.3 us (24%)
  Pallas kernels  14.1 us (10%)
  starting transfers between devices  11 us (8%)
  local copies, waits for them, and re-layouts  2.17 us (2%)
    all_to_all x1, blocking collectives, local(): gathered = lax.all_to_all(spread, KEY_AXES, 0, 0, tiled=True)  34.9 us
    all_to_all x1, blocking collectives, local(): back = lax.all_to_all(grads, HEAD_AXES, 0, 0, tiled=True)  24.5 us
    all_to_all x1, waiting for transfers between devices, local(): held = lax.all_to_all(packed, HEAD_AXES, 0, 0, tiled=True)  21.9 us
    all_to_all x1, blocking collectives, local(): stats = lax.all_to_all(stats, KEY_AXES, 0, 0, tiled=True)  16.7 us
    all_to_all x1, waiting for transfers between devices, local(): parts = lax.all_to_all(parts, KEY_AXES, 0, 0, tiled=True)  12.4 us
    all_to_all x1, starting transfers between devices, local(): held = lax.all_to_all(packed, HEAD_AXES, 0, 0, tiled=True)  7.5 us
    pallas_call x1, Pallas kernels, local(): call(grads_kernel, 'grads', shape((HEADS, BACK, DH), bf16), queries + [pl...  6.46 us
    pallas_call x1, Pallas kernels, local(): call(stats_kernel, 'stats', shape((GROUPS, 8, 256), f32), queries + sums,...  3.65 us
  transfers between devices with their start and end apart: 2, of which 2 were waited for; matrix products, arithmetic and copies ran while one was open for 1% of the time, Pallas kernels for 1%

profile of v1, /device:TPU:1, one launch (start us, length us, event | category | flops | bytes accessed | tf_op | source)
XLA Modules:
  0.0 139.6 jit_solution(14039776144817847021)
XLA Ops:
  0.6 0.0 copy-start
  0.6 0.0 copy-start.2
  0.7 0.0 copy-start.1
  0.7 0.0 copy-start.3
  0.7 0.0 copy-start.4
  0.7 0.8 copy-done.4
  1.5 0.0 copy-start.5
  1.5 0.7 copy-done.5
  2.2 0.1 spread.1
  2.2 34.9 %all_to_all.35 = bf16[16,8,2048]{2,1,0:T(8,128)(2,1)S(1)} all-to-all(bf16[16,8,2048]{2,1,0:T(8,128)(2,1)S(1)} %bitcast.7), channel_id=1, replica_groups=mesh['zh'=4,'zl'=2,'ym'=2,'yl'=2,'x'=4,'yh'=2,'core'=2] {'zh','ym','yh'}, dimensions={0} | all-to-all | bytes 1048576 | tf_op jit(solution)/shard_map/all_to_all | solution.py:248
  37.2 0.0 copy-done
  37.2 0.0 copy-done.2
  37.2 0.0 copy-done.1
  37.2 0.0 copy-done.3
  37.2 1.6 %pack.1 = bf16[32,192,128]{2,1,0:T(8,128)(2,1)} custom-call(bf16[128,2048]{1,0:T(8,128)(2,1)S(1)} %bitcast.6, bf16[62,4096]{1,0:T(8,128)(2,1)S(1)} %copy-done, bf16[2,4096]{1,0:T(2,128)(2,1)S(1)} %copy-done.2, bf16[62,4096]{1,0:T(8,128)(2,1)S(1)} %copy-done.1, bf16[2,4096]{1,0:T(2,128)(2,1)S(1)} %copy-done.3), custom_call_target="tpu_custom_call" | custom-call | bytes 2097152 | tf_op jit(solution)/shard_map/pack/pallas_call | solution.py:249
  38.8 0.0 copy-start.7
  38.8 0.0 copy-start.6
  38.8 7.5 %all-to-all-start.1 = ((bf16[32,192,128]{2,1,0:T(8,128)(2,1)}), bf16[32,192,128]{2,1,0:T(8,128)(2,1)S(1)}, u32[]{:S(2)}, u32[]{:S(2)}) async-start(bf16[32,192,128]{2,1,0:T(8,128)(2,1)} %pack.1), calls=%async_computation.1 | async-start | bytes 3145728 | tf_op jit(solution)/shard_map/all_to_all | solution.py:252
  46.4 0.0 copy-done.7
  46.4 0.1 compare_reduce_fusion
  46.5 0.0 copy-done.6
  46.5 0.8 fusion.1.mask_ref
  47.3 21.9 %all-to-all-done.1.in_ref = bf16[32,192,128]{2,1,0:T(8,128)(2,1)S(1)} async-done(((bf16[32,192,128]{2,1,0:T(8,128)(2,1)}), bf16[32,192,128]{2,1,0:T(8,128)(2,1)S(1)}, u32[]{:S(2)}, u32[]{:S(2)}) %all-to-all-start.1) | async-done | bytes 1572896 | tf_op jit(solution)/shard_map/all_to_all | solution.py:252
  69.2 3.7 %stats.1 = f32[16,8,256]{2,1,0:T(8,128)S(1)} custom-call(bf16[32,192,128]{2,1,0:T(8,128)(2,1)S(1)} %all-to-all-done.1.in_ref, bf16[2048,128]{1,0:T(8,128)(2,1)S(1)} %fusion.1.mask_ref), custom_call_target="tpu_custom_call" | custom-call | flops 1610612736 | bytes 2097152 | tf_op jit(solution)/shard_map/stats/pallas_call | solution.py:255
  72.8 16.7 %all_to_all.36.stats_ref = f32[16,8,256]{2,1,0:T(8,128)S(1)} all-to-all(f32[16,8,256]{2,1,0:T(8,128)S(1)} %stats.1), channel_id=1, replica_groups=mesh['zh'=4,'zl'=2,'ym'=2,'yl'=2,'x'=4,'yh'=2,'core'=2] {'zh','ym','yh'}, dimensions={0} | all-to-all | bytes 262144 | tf_op jit(solution)/shard_map/all_to_all | solution.py:263
  89.6 6.5 %grads.1 = bf16[32,160,128]{2,1,0:T(8,128)(2,1)S(1)} custom-call(bf16[32,192,128]{2,1,0:T(8,128)(2,1)S(1)} %all-to-all-done.1.in_ref, bf16[2048,128]{1,0:T(8,128)(2,1)S(1)} %fusion.1.mask_ref, f32[16,8,256]{2,1,0:T(8,128)S(1)} %all_to_all.36.stats_ref), custom_call_target="tpu_custom_call" | custom-call | flops 3221225472 | bytes 2097152 | tf_op jit(solution)/shard_map/grads/pallas_call | solution.py:264
  96.0 24.5 %all_to_all.37.back_ref = bf16[32,160,128]{2,1,0:T(8,128)(2,1)S(1)} all-to-all(bf16[32,160,128]{2,1,0:T(8,128)(2,1)S(1)} %grads.1), channel_id=1, replica_groups=mesh['zh'=4,'zl'=2,'ym'=2,'yl'=2,'x'=4,'yh'=2,'core'=2] {'zl','yl','x','..., dimensions={0} | all-to-all | bytes 2621440 | tf_op jit(solution)/shard_map/all_to_all | solution.py:273
  120.6 0.9 unpack_queries.1
  121.5 3.5 %all-to-all-start.4 = ((bf16[16,8,1024]{2,1,0:T(8,128)(2,1)}), bf16[16,8,1024]{2,1,0:T(8,128)(2,1)S(1)}, u32[]{:S(2)}, u32[]{:S(2)}) async-start(bf16[16,8,1024]{2,1,0:T(8,128)(2,1)} %bitcast.2), calls=%async_computation.4 | async-start | bytes 524288 | tf_op jit(solution)/shard_map/all_to_all | solution.py:275
  125.0 1.4 %unpack_keys.1 = (f32[62,4096]{1,0:T(8,128)}, f32[62,4096]{1,0:T(8,128)}, f32[2,4096]{1,0:T(2,128)}, f32[2,4096]{1,0:T(2,128)}) custom-call(bf16[32,160,128]{2,1,0:T(8,128)(2,1)S(1)} %all_to_all.37.back_ref), custom_call_target="tpu_custom_call" | custom-call | bytes 4194304 | tf_op jit(solution)/shard_map/unpack_keys/pallas_call | solution.py:276
  126.5 12.4 %all-to-all-done.4 = bf16[16,8,1024]{2,1,0:T(8,128)(2,1)S(1)} async-done(((bf16[16,8,1024]{2,1,0:T(8,128)(2,1)}), bf16[16,8,1024]{2,1,0:T(8,128)(2,1)S(1)}, u32[]{:S(2)}, u32[]{:S(2)}) %all-to-all-start.4) | async-done | bytes 262176 | tf_op jit(solution)/shard_map/all_to_all | solution.py:275
  138.9 0.6 reduce_sum.12
  (6 shorter events, 0.1 us)
Async XLA Ops:
  0.6 36.5 %copy-start = (bf16[62,4096]{1,0:T(8,128)(2,1)S(1)}, bf16[62,4096]{1,0:T(8,128)(2,1)}, u32[]{:S(2)}) copy-start(bf16[62,4096]{1,0:T(8,128)(2,1)} %mem_k_ref.1) | copy-start | bytes 1523716
  0.6 36.5 %copy-start.2 = (bf16[2,4096]{1,0:T(2,128)(2,1)S(1)}, bf16[2,4096]{1,0:T(2,128)(2,1)}, u32[]{:S(2)}) copy-start(bf16[2,4096]{1,0:T(2,128)(2,1)} %span_k_ref.1) | copy-start | bytes 49156
  0.7 36.5 %copy-start.1 = (bf16[62,4096]{1,0:T(8,128)(2,1)S(1)}, bf16[62,4096]{1,0:T(8,128)(2,1)}, u32[]{:S(2)}) copy-start(bf16[62,4096]{1,0:T(8,128)(2,1)} %mem_v_ref.1) | copy-start | bytes 1523716
  0.7 36.5 %copy-start.3 = (bf16[2,4096]{1,0:T(2,128)(2,1)S(1)}, bf16[2,4096]{1,0:T(2,128)(2,1)}, u32[]{:S(2)}) copy-start(bf16[2,4096]{1,0:T(2,128)(2,1)} %span_v_ref.1) | copy-start | bytes 49156
  0.7 0.8 copy-start.4
  1.5 0.7 copy-start.5
  38.8 7.6 %copy-start.7 = (s32[2,32]{1,0:T(2,128)S(1)}, s32[2,32]{1,0:T(2,128)}, u32[]{:S(2)}) copy-start(s32[2,32]{1,0:T(2,128)} %param.14) | copy-start | bytes 772
  38.8 7.7 %copy-start.6 = (s32[2,248]{1,0:T(2,128)S(1)}, s32[2,248]{1,0:T(2,128)}, u32[]{:S(2)}) copy-start(s32[2,248]{1,0:T(2,128)} %param.15) | copy-start | bytes 5956
  38.8 30.4 %all-to-all-start.1 = ((bf16[32,192,128]{2,1,0:T(8,128)(2,1)}), bf16[32,192,128]{2,1,0:T(8,128)(2,1)S(1)}, u32[]{:S(2)}, u32[]{:S(2)}) async-start(bf16[32,192,128]{2,1,0:T(8,128)(2,1)} %pack.1), calls=%async_computation.1 | async-start | bytes 3145728 | tf_op jit(solution)/shard_map/all_to_all | solution.py:252
  121.5 17.4 %all-to-all-start.4 = ((bf16[16,8,1024]{2,1,0:T(8,128)(2,1)}), bf16[16,8,1024]{2,1,0:T(8,128)(2,1)S(1)}, u32[]{:S(2)}, u32[]{:S(2)}) async-start(bf16[16,8,1024]{2,1,0:T(8,128)(2,1)} %bitcast.2), calls=%async_computation.4 | async-start | bytes 524288 | tf_op jit(solution)/shard_map/all_to_all | solution.py:275

commit v2 on v1

--- a/solution.py
+++ b/solution.py
@@ -1,3 +1,4 @@
+import functools
 import math
 
 import jax
@@ -24,12 +25,16 @@
 HEAD_AXES = ("zl", "yl", "x", "core")
 KEY_AXES = ("zh", "ym", "yh")
 GROUPS = 16
+HALF_GROUPS = GROUPS // QF
+NEAR_AXES, NEAR = ("ym", "yh"), 4
+FAR_AXES, FAR = ("zh",), 4
 
 HALF = FRAME // HEADS
 CHUNK = 512
 SOURCES = CHUNK // ROWS
-K_AT, V_AT, Q_AT, G_AT = 0, ROWS, 2 * ROWS, 2 * ROWS + 2 * HALF
-SENT = 2 * ROWS + 4 * HALF
+BLOCK = HEADS * SPAN_ROWS
+K_AT, V_AT, Q_AT = 0, ROWS, 2 * ROWS
+SENT = 2 * ROWS
 BACK = 2 * ROWS + 2 * HALF
 WIDE = HEADS * DH // 2
 LOG2E = math.log2(math.e)
@@ -38,14 +43,16 @@
 FLOOR = -1e20
 
 
-def load_queries(in_ref, qt_ref, gt_ref):
+def load_queries(qg_ref, qt_ref, gt_ref):
     pick = lax.broadcasted_iota(jnp.int32, (DH, FRAME), 0)
     for f in range(QF):
-        q = in_ref[:, Q_AT + f * HALF : Q_AT + (f + 1) * HALF, :].reshape(FRAME, DH)
-        g = in_ref[:, G_AT + f * HALF : G_AT + (f + 1) * HALF, :].reshape(FRAME, DH)
-        qt_ref[f, 0:DH, :] = q.T
+        qt_ref[f, 0:DH, :] = frame_rows(qg_ref, 0, f).T
         qt_ref[f, DH : 2 * DH, :] = jnp.where(pick == f, 1.0, 0.0).astype(jnp.bfloat16)
-        gt_ref[f] = g.T
+        gt_ref[f] = frame_rows(qg_ref, 1, f).T
+
+
+def frame_rows(qg_ref, which, f):
+    return qg_ref[which, f * HALF_GROUPS : (f + 1) * HALF_GROUPS, :, :].reshape(FRAME, DH)
 
 
 def load_keys(in_ref, mask_ref, c):
@@ -61,8 +68,14 @@
     return jnp.dot(a, b, preferred_element_type=jnp.float32)
 
 
-def stats_kernel(in_ref, mask_ref, out_ref, qt_ref, gt_ref, max_ref, sum_ref, dot_ref):
-    load_queries(in_ref, qt_ref, gt_ref)
+def stats_kernel(group_ref, in_ref, mask_ref, *refs):
+    blocks = refs[:FAR]
+    out_ref, qg_ref, qt_ref, gt_ref, max_ref, sum_ref, dot_ref = refs[FAR:]
+    for j in range(GROUPS):
+        group = group_ref[0] ^ j
+        qg_ref[0, group] = blocks[j // NEAR][j % NEAR, :BLOCK, :]
+        qg_ref[1, group] = blocks[j // NEAR][j % NEAR, BLOCK:, :]
+    load_queries(qg_ref, qt_ref, gt_ref)
     max_ref[...] = jnp.full(max_ref.shape, FLOOR, jnp.float32)
     sum_ref[...] = jnp.zeros(sum_ref.shape, jnp.float32)
     dot_ref[...] = jnp.zeros(dot_ref.shape, jnp.float32)
@@ -94,20 +107,29 @@
         mean_row = inner / safe
         logs += [log_row[:, :256], log_row[:, 256:]]
         means += [mean_row[:, :256], mean_row[:, 256:]]
-    stats = jnp.concatenate(logs + means, axis=0)
-    out_ref[...] = jnp.broadcast_to(stats[None], out_ref.shape)
-
-
-def grads_kernel(in_ref, mask_ref, stats_ref, out_ref, qt_ref, gt_ref, acc_ref):
-    load_queries(in_ref, qt_ref, gt_ref)
+    out_ref[...] = jnp.concatenate(logs + means, axis=0)
+
+
+def merged(stats_refs):
+    logs = [ref[0:4, :] for ref in stats_refs]
+    top = functools.reduce(jnp.maximum, logs)
+    weights = [jnp.exp2(log - top) for log in logs]
+    total = sum(weights)
+    means = sum(weight * ref[4:8, :] for weight, ref in zip(weights, stats_refs))
+    return top + jnp.log(total) * LOG2E, means / total
+
+
+def merge_kernel(*refs):
+    log_total, mean = merged(refs[:-1])
+    refs[-1][...] = jnp.concatenate([log_total, mean], axis=0)
+
+
+def grads_kernel(in_ref, mask_ref, qg_ref, *refs):
+    stats_refs = refs[:FAR]
+    out_ref, qt_ref, gt_ref, acc_ref = refs[FAR:]
+    load_queries(qg_ref, qt_ref, gt_ref)
     acc_ref[...] = jnp.zeros(acc_ref.shape, jnp.float32)
-    logs = stats_ref[:, 0:4, :]
-    means = stats_ref[:, 4:8, :]
-    top = jnp.max(logs, axis=0)
-    weights = jnp.exp2(logs - top[None])
-    total = jnp.sum(weights, axis=0)
-    log_total = top + jnp.log(total) * LOG2E
-    delta = jnp.sum(weights * means, axis=0) / total
+    log_total, delta = merged(stats_refs)
 
     def row(stat, f):
         return jnp.concatenate([stat[2 * f : 2 * f + 1], stat[2 * f + 1 : 2 * f + 2]], axis=1)
@@ -121,8 +143,7 @@
         key_grad = jnp.zeros((CHUNK, DH), jnp.float32)
         value_grad = jnp.zeros((CHUNK, DH), jnp.float32)
         for f in range(QF):
-            q = in_ref[:, Q_AT + f * HALF : Q_AT + (f + 1) * HALF, :].reshape(FRAME, DH)
-            g = in_ref[:, G_AT + f * HALF : G_AT + (f + 1) * HALF, :].reshape(FRAME, DH)
+            q, g = frame_rows(qg_ref, 0, f), frame_rows(qg_ref, 1, f)
             scores = dot(masked_keys, qt_ref[f]) * (SCALE * LOG2E)
             probs = jnp.exp2(scores - log_rows[f])
             products = dot(values, gt_ref[f])
@@ -141,7 +162,10 @@
 
     lax.fori_loop(0, HEADS * ROWS // CHUNK, visit, 0)
     for f in range(QF):
-        query_grad = (acc_ref[f].T * SCALE).astype(jnp.bfloat16)
+        query_grad = moved(
+            lambda i: (i // 2 % HALF_GROUPS) * BLOCK + (i // HALF) * 2 + i % 2,
+            (acc_ref[f] * SCALE).astype(jnp.bfloat16).T,
+        )
         out_ref[:, Q_AT + f * HALF : Q_AT + (f + 1) * HALF, :] = query_grad.reshape(HEADS, HALF, DH)
 
 
@@ -170,35 +194,32 @@
     return jnp.where(hit > 0.5, BARRED, 0.0).astype(jnp.bfloat16)
 
 
-def spread_kernel(q_ref, g_ref, out_ref):
-    rows = jnp.concatenate(
-        [part[:, half] for part in (q_ref, g_ref) for half in (slice(0, WIDE), slice(WIDE, 2 * WIDE))],
-        axis=0,
-    )
-    for b in range(0, GROUPS, 2):
-        out_ref[8 * b : 8 * (b + 2), :] = jnp.concatenate([rows, rows], axis=0)
-
-
-def moved(order, rows):
-    count = rows.shape[0]
-    to = lax.broadcasted_iota(jnp.int32, (count, count), 0)
-    at = lax.broadcasted_iota(jnp.int32, (count, count), 1)
+def split_kernel(q_ref, g_ref, out_ref):
+    rows = jnp.concatenate([q_ref[...], g_ref[...], q_ref[...], g_ref[...]], axis=0)
+    for h in range(HEADS):
+        out_ref[h] = rows[:, h * DH : (h + 1) * DH]
+
+
+def moved(order, rows, count=None):
+    dims = (count or rows.shape[0], rows.shape[0])
+    to = lax.broadcasted_iota(jnp.int32, dims, 0)
+    at = lax.broadcasted_iota(jnp.int32, dims, 1)
     pick = jnp.where(order(to) == at, 1.0, 0.0).astype(jnp.bfloat16)
     return dot(pick, rows).astype(jnp.bfloat16)
 
 
-def pack_kernel(gathered_ref, mem_k_ref, span_k_ref, mem_v_ref, span_v_ref, out_ref):
-    rows = moved(
-        lambda i: (i // 2 % 16) * 8 + (i // 32 % 2) * 4 + (i // 64) * 2 + i % 2, gathered_ref[...]
-    )
+def block_kernel(in_ref, out_ref):
+    rows = in_ref[...].reshape(8 * HEADS, DH)
+    out_ref[...] = moved(lambda i: (i // 2 % HEADS) * 8 + (i // BLOCK) * 2 + i % 2, rows, 2 * BLOCK)
+
+
+def pack_kernel(mem_k_ref, span_k_ref, mem_v_ref, span_v_ref, out_ref):
     for h in range(HEADS):
         lanes = slice(h * DH, (h + 1) * DH)
         out_ref[h, K_AT : K_AT + MEM_ROWS, :] = mem_k_ref[:, lanes]
         out_ref[h, K_AT + MEM_ROWS : K_AT + ROWS, :] = span_k_ref[:, lanes]
         out_ref[h, V_AT : V_AT + MEM_ROWS, :] = mem_v_ref[:, lanes]
         out_ref[h, V_AT + MEM_ROWS : V_AT + ROWS, :] = span_v_ref[:, lanes]
-        half, at = divmod(h * DH, WIDE)
-        out_ref[h, Q_AT:SENT, :] = rows[half * 4 * HALF : (half + 1) * 4 * HALF, at : at + DH]
 
 
 def unpack_queries_kernel(back_ref, out_ref):
@@ -221,9 +242,11 @@
         span_v_ref[:, lanes] = value_grad[MEM_ROWS:]
 
 
-def call(kernel, name, out_shape, scratch_shapes=(), flops=0, transcendentals=0, moved_bytes=2 << 20):
+def call(kernel, name, out_shape, scratch_shapes=(), flops=0, transcendentals=0, moved_bytes=2 << 20, scalars=0, arrays=1):
     return pl.pallas_call(
         kernel,
+        in_specs=[pl.BlockSpec(memory_space=pltpu.SMEM)] * scalars
+        + [pl.BlockSpec(memory_space=pltpu.VMEM)] * arrays,
         out_shape=out_shape,
         scratch_shapes=list(scratch_shapes),
         compiler_params=pltpu.CompilerParams(vmem_limit_bytes=40 * 1024 * 1024),
@@ -234,6 +257,12 @@
     )
 
 
+def swaps(array, axes, size):
+    return [array] + [
+        lax.ppermute(array, axes, [(i, i ^ j) for i in range(size)]) for j in range(1, size)
+    ]
+
+
 def shape(dims, dtype):
     return jax.ShapeDtypeStruct(dims, dtype)
 
@@ -244,23 +273,32 @@
     queries = [pltpu.VMEM((QF, 2 * DH, FRAME), bf16), pltpu.VMEM((QF, DH, FRAME), bf16)]
     sums = [pltpu.VMEM((QF, 8, FRAME), f32)] * 3
 
-    spread = call(spread_kernel, "spread", shape((8 * GROUPS, WIDE), bf16))(span_q, span_grad)
-    gathered = lax.all_to_all(spread, KEY_AXES, 0, 0, tiled=True)
-    packed = call(pack_kernel, "pack", shape((HEADS, SENT, DH), bf16))(
-        gathered, mem_k, span_k, mem_v, span_v
+    split = call(split_kernel, "split", shape((HEADS, 8, DH), bf16), arrays=2)(span_q, span_grad)
+    split = lax.all_to_all(split, HEAD_AXES, 0, 0, tiled=True)
+    block = call(block_kernel, "block", shape((2 * BLOCK, DH), bf16))(split)
+    near = jnp.stack(swaps(block, NEAR_AXES, NEAR))
+    blocks = swaps(near, FAR_AXES, FAR)
+    packed = call(pack_kernel, "pack", shape((HEADS, SENT, DH), bf16), arrays=4)(
+        mem_k, span_k, mem_v, span_v
     )
     held = lax.all_to_all(packed, HEAD_AXES, 0, 0, tiled=True)
 
     mask = mask_rows(retrieved, tile_keep)
-    stats = call(
+    group = lax.axis_index(KEY_AXES).astype(jnp.int32).reshape(1)
+    stats, queries_grads = call(
         stats_kernel,
         "stats",
-        shape((GROUPS, 8, 256), f32),
+        (shape((8, 256), f32), shape((2, GROUPS, BLOCK, DH), bf16)),
         queries + sums,
         flops=6 * pairs * DH,
         transcendentals=pairs,
-    )(held, mask)
-    stats = lax.all_to_all(stats, KEY_AXES, 0, 0, tiled=True)
+        scalars=1,
+        arrays=2 + FAR,
+    )(group, held, mask, *blocks)
+    near_stats = call(merge_kernel, "merge", shape((8, 256), f32), arrays=NEAR)(
+        *swaps(stats, NEAR_AXES, NEAR)
+    )
+    all_stats = swaps(near_stats, FAR_AXES, FAR)
     grads = call(
         grads_kernel,
         "grads",
@@ -268,7 +306,8 @@
         queries + [pltpu.VMEM((QF, DH, FRAME), f32)],
         flops=12 * pairs * DH,
         transcendentals=pairs,
-    )(held, mask, stats)
+        arrays=3 + FAR,
+    )(held, mask, queries_grads, *all_stats)
 
     back = lax.all_to_all(grads, HEAD_AXES, 0, 0, tiled=True)
     parts = call(unpack_queries_kernel, "unpack_queries", shape((8 * GROUPS, WIDE // 2), bf16))(back)

time: 140 us -> 162 us (1.16)
  starting transfers between devices: 11 us -> 73.7 us
  blocking collectives: 76.2 us -> 29.6 us
  local copies, waits for them, and re-layouts: 2.17 us -> 5.58 us
    all_to_all x2 -> x0, blocking collectives: 51.6 us -> none  [the longest x1 34.9 us: local(): gathered = lax.all_to_all(spread, KEY_AXES, 0, 0, tiled=True)]
    ppermute x0 -> x12, starting transfers between devices: none -> 49.8 us  [swaps(): lax.ppermute(array, axes, [(i, i ^ j) for i in range(size)])]
    all_to_all x1, waiting for transfers between devices: 21.9 us -> 0.01 us  [local(): held = lax.all_to_all(packed, HEAD_AXES, 0, 0, tiled=True)]
    ppermute x0 -> x12, waiting for transfers between devices: none -> 20.6 us  [swaps(): lax.ppermute(array, axes, [(i, i ^ j) for i in range(size)])]
    all_to_all x0 -> x1, starting transfers between devices: none -> 10.4 us  [local(): split = lax.all_to_all(split, HEAD_AXES, 0, 0, tiled=True)]
    all_to_all x1, starting transfers between devices: 3.53 us -> 8.66 us  [local(): parts = lax.all_to_all(parts, KEY_AXES, 0, 0, tiled=True)]
    all_to_all x1, blocking collectives: 24.5 us -> 29.6 us  [local(): back = lax.all_to_all(grads, HEAD_AXES, 0, 0, tiled=True)]
    unnamed x16, local copies, waits for them, and re-layouts: 1.53 us -> 4.95 us
  transfers between devices with their start and end apart: 2 -> 15, of which waited for: 2 -> 9; matrix products, arithmetic and copies ran while one was open for 1% -> 1% of each run, Pallas kernels for 1% -> 2%
where the time goes in v2:
time: 162 us; the launch traced here: 160 us
  starting transfers between devices  73.7 us (45%)
  waiting for transfers between devices  34.6 us (21%)
  blocking collectives  29.6 us (18%)
  Pallas kernels  14.8 us (9%)
  local copies, waits for them, and re-layouts  5.58 us (3%)
    ppermute x12, starting transfers between devices, swaps(): lax.ppermute(array, axes, [(i, i ^ j) for i in range(size)])  49.8 us
    all_to_all x1, blocking collectives, local(): back = lax.all_to_all(grads, HEAD_AXES, 0, 0, tiled=True)  29.6 us
    ppermute x12, waiting for transfers between devices, swaps(): lax.ppermute(array, axes, [(i, i ^ j) for i in range(size)])  20.6 us
    all_to_all x1, waiting for transfers between devices, local(): parts = lax.all_to_all(parts, KEY_AXES, 0, 0, tiled=True)  11.8 us
    all_to_all x1, starting transfers between devices, local(): split = lax.all_to_all(split, HEAD_AXES, 0, 0, tiled=True)  10.4 us
    all_to_all x1, starting transfers between devices, local(): parts = lax.all_to_all(parts, KEY_AXES, 0, 0, tiled=True)  8.66 us
    pallas_call x1, Pallas kernels, local(): call(grads_kernel, 'grads', shape((HEADS, BACK, DH), bf16), queries + [pl...  6.72 us
    unnamed x16, local copies, waits for them, and re-layouts  4.95 us
  transfers between devices with their start and end apart: 15, of which 9 were waited for; matrix products, arithmetic and copies ran while one was open for 1% of the time, Pallas kernels for 2%

profile of v2, /device:TPU:1, one launch (start us, length us, event | category | flops | bytes accessed | tf_op | source)
XLA Modules:
  0.0 160.2 jit_solution(8602675482086635240)
XLA Ops:
  0.6 0.0 copy-start.4
  0.6 0.7 copy-done.4
  1.3 0.0 copy-start.5
  1.4 0.7 copy-done.5
  2.1 0.7 split.1
  2.7 10.4 %all-to-all-start.1 = ((bf16[32,8,128]{2,1,0:T(8,128)(2,1)}), bf16[32,8,128]{2,1,0:T(8,128)(2,1)S(1)}, u32[]{:S(2)}, u32[]{:S(2)}) async-start(bf16[32,8,128]{2,1,0:T(8,128)(2,1)} %split.1), calls=%async_computation.1 | async-start | bytes 131072 | tf_op jit(solution)/shard_map/all_to_all | solution.py:277
  13.1 0.0 copy-start
  13.1 1.0 copy-done
  14.2 0.0 copy-start.1
  14.2 1.0 copy-done.1
  15.2 0.0 copy-start.2
  15.2 0.7 copy-done.2
  15.9 0.0 copy-start.3
  15.9 0.7 copy-done.3
  16.7 1.2 pack.1
  17.9 0.0 copy-start.7
  17.9 0.0 copy-start.6
  17.9 2.2 %all-to-all-done.1.in_ref = bf16[32,8,128]{2,1,0:T(8,128)(2,1)S(1)} async-done(((bf16[32,8,128]{2,1,0:T(8,128)(2,1)}), bf16[32,8,128]{2,1,0:T(8,128)(2,1)S(1)}, u32[]{:S(2)}, u32[]{:S(2)}) %all-to-all-start.1) | async-done | bytes 65568 | tf_op jit(solution)/shard_map/all_to_all | solution.py:277
  20.0 4.9 %all-to-all-start = ((bf16[32,128,128]{2,1,0:T(8,128)(2,1)}), bf16[32,128,128]{2,1,0:T(8,128)(2,1)S(1)}, u32[]{:S(2)}, u32[]{:S(2)}) async-start(bf16[32,128,128]{2,1,0:T(8,128)(2,1)} %pack.1), calls=%async_computation | async-start | bytes 2097152 | tf_op jit(solution)/shard_map/all_to_all | solution.py:284
  25.0 0.0 copy-done.7
  25.0 0.1 compare_reduce_fusion
  25.1 0.0 copy-done.6
  25.1 0.1 block.1
  25.3 3.3 %collective-permute-start.2 = (bf16[128,128]{1,0:T(8,128)(2,1)S(1)}, bf16[128,128]{1,0:T(8,128)(2,1)S(1)}, u32[]{:S(2)}, u32[]{:S(2)}) collective-permute-start(bf16[128,128]{1,0:T(8,128)(2,1)S(1)} %block.1), channel_id=1, source_target_pairs={{0,34},{2,32},{32,2},{34,0},{1,35},{3,33},{33,3},{35,1},{4,38},{6,... | collective-permute-start | bytes 98312 | tf_op jit(solution)/shard_map/ppermute | solution.py:262
  28.5 3.8 %collective-permute-start.1 = (bf16[128,128]{1,0:T(8,128)(2,1)S(1)}, bf16[128,128]{1,0:T(8,128)(2,1)S(1)}, u32[]{:S(2)}, u32[]{:S(2)}) collective-permute-start(bf16[128,128]{1,0:T(8,128)(2,1)S(1)} %block.1), channel_id=1, source_target_pairs={{0,32},{2,34},{32,0},{34,2},{1,33},{3,35},{33,1},{35,3},{4,36},{6,... | collective-permute-start | bytes 98312 | tf_op jit(solution)/shard_map/ppermute | solution.py:262
  32.3 4.4 %collective-permute-start = (bf16[128,128]{1,0:T(8,128)(2,1)S(1)}, bf16[128,128]{1,0:T(8,128)(2,1)S(1)}, u32[]{:S(2)}, u32[]{:S(2)}) collective-permute-start(bf16[128,128]{1,0:T(8,128)(2,1)S(1)} %block.1), channel_id=1, source_target_pairs={{0,2},{2,0},{32,34},{34,32},{1,3},{3,1},{33,35},{35,33},{4,6},{6,4... | collective-permute-start | bytes 98312 | tf_op jit(solution)/shard_map/ppermute | solution.py:262
  36.7 3.3 %collective-permute-done.2 = bf16[128,128]{1,0:T(8,128)(2,1)S(1)} collective-permute-done((bf16[128,128]{1,0:T(8,128)(2,1)S(1)}, bf16[128,128]{1,0:T(8,128)(2,1)S(1)}, u32[]{:S(2)}, u32[]{:S(2)}) %collective-permute-start.2) | collective-permute-done | bytes 32800 | tf_op jit(solution)/shard_map/ppermute | solution.py:262
  40.0 0.0 collective-permute-done.1
  40.0 2.3 %collective-permute-done = bf16[128,128]{1,0:T(8,128)(2,1)S(1)} collective-permute-done((bf16[128,128]{1,0:T(8,128)(2,1)S(1)}, bf16[128,128]{1,0:T(8,128)(2,1)S(1)}, u32[]{:S(2)}, u32[]{:S(2)}) %collective-permute-start) | collective-permute-done | bytes 32800 | tf_op jit(solution)/shard_map/ppermute | solution.py:262
  42.3 9.7 %collective-permute-start.5 = (bf16[4,128,128]{2,1,0:T(8,128)(2,1)S(1)}, bf16[4,128,128]{2,1,0:T(8,128)(2,1)S(1)}, u32[]{:S(2)}, u32[]{:S(2)}) collective-permute-start(bf16[4,128,128]{2,1,0:T(8,128)(2,1)S(1)} %pad_maximum_fusion.refs_0_), channel_id=1, source_target_pairs={{0,384},{128,256},{256,128},{384,0},{1,385},{129,257},{257,129},{3... | collective-permute-start | bytes 393224 | tf_op jit(solution)/shard_map/ppermute | solution.py:262
  52.0 1.9 %collective-permute-start.4 = (bf16[4,128,128]{2,1,0:T(8,128)(2,1)S(1)}, bf16[4,128,128]{2,1,0:T(8,128)(2,1)S(1)}, u32[]{:S(2)}, u32[]{:S(2)}) collective-permute-start(bf16[4,128,128]{2,1,0:T(8,128)(2,1)S(1)} %pad_maximum_fusion.refs_0_), channel_id=1, source_target_pairs={{0,256},{128,384},{256,0},{384,128},{1,257},{129,385},{257,1},{385... | collective-permute-start | bytes 393224 | tf_op jit(solution)/shard_map/ppermute | solution.py:262
  54.0 4.0 %collective-permute-start.3 = (bf16[4,128,128]{2,1,0:T(8,128)(2,1)S(1)}, bf16[4,128,128]{2,1,0:T(8,128)(2,1)S(1)}, u32[]{:S(2)}, u32[]{:S(2)}) collective-permute-start(bf16[4,128,128]{2,1,0:T(8,128)(2,1)S(1)} %pad_maximum_fusion.refs_0_), channel_id=1, source_target_pairs={{0,128},{128,0},{256,384},{384,256},{1,129},{129,1},{257,385},{385... | collective-permute-start | bytes 393224 | tf_op jit(solution)/shard_map/ppermute | solution.py:262
  58.0 0.8 fusion.1.mask_ref
  58.7 4.0 %collective-permute-done.5.refs_3_ = bf16[4,128,128]{2,1,0:T(8,128)(2,1)S(1)} collective-permute-done((bf16[4,128,128]{2,1,0:T(8,128)(2,1)S(1)}, bf16[4,128,128]{2,1,0:T(8,128)(2,1)S(1)}, u32[]{:S(2)}, u32[]{:S(2)}) %collective-permute-start.5) | collective-permute-done | bytes 131104 | tf_op jit(solution)/shard_map/ppermute | solution.py:262
  62.7 4.3 %collective-permute-done.4.refs_2_ = bf16[4,128,128]{2,1,0:T(8,128)(2,1)S(1)} collective-permute-done((bf16[4,128,128]{2,1,0:T(8,128)(2,1)S(1)}, bf16[4,128,128]{2,1,0:T(8,128)(2,1)S(1)}, u32[]{:S(2)}, u32[]{:S(2)}) %collective-permute-start.4) | collective-permute-done | bytes 131104 | tf_op jit(solution)/shard_map/ppermute | solution.py:262
  67.1 3.0 %collective-permute-done.3.refs_1_ = bf16[4,128,128]{2,1,0:T(8,128)(2,1)S(1)} collective-permute-done((bf16[4,128,128]{2,1,0:T(8,128)(2,1)S(1)}, bf16[4,128,128]{2,1,0:T(8,128)(2,1)S(1)}, u32[]{:S(2)}, u32[]{:S(2)}) %collective-permute-start.3) | collective-permute-done | bytes 131104 | tf_op jit(solution)/shard_map/ppermute | solution.py:262
  70.1 0.0 all-to-all-done.in_ref
  70.1 3.7 %stats.1 = (f32[8,256]{1,0:T(8,128)S(1)}, bf16[2,16,64,128]{3,2,1,0:T(8,128)(2,1)S(1)}) custom-call(s32[1]{0:T(128)} %bitcast.group_ref, bf16[32,128,128]{2,1,0:T(8,128)(2,1)S(1)} %all-to-all-done.in_ref, bf16[2048,128]{1,0:T(8,128)(2,1)S(1)} %fusion.1.mask_ref, bf16[4,128,128]{2,1,0:T(8,128)(2,1)S(1)} %pad_maximum_fusion.refs_0_, ...), custom_call_target="tpu_custom_call" | custom-call | flops 1610612736 | bytes 2097152 | tf_op jit(solution)/shard_map/stats/pallas_call | solution.py:288
  73.8 3.6 %collective-permute-start.8 = (f32[8,256]{1,0:T(8,128)S(1)}, f32[8,256]{1,0:T(8,128)S(1)}, u32[]{:S(2)}, u32[]{:S(2)}) collective-permute-start(f32[8,256]{1,0:T(8,128)S(1)} %get-tuple-element.12.refs_0_), channel_id=1, source_target_pairs={{0,34},{2,32},{32,2},{34,0},{1,35},{3,33},{33,3},{35,1},{4,38},{6,... | collective-permute-start | bytes 24584 | tf_op jit(solution)/shard_map/ppermute | solution.py:262
  77.3 1.9 %collective-permute-start.7 = (f32[8,256]{1,0:T(8,128)S(1)}, f32[8,256]{1,0:T(8,128)S(1)}, u32[]{:S(2)}, u32[]{:S(2)}) collective-permute-start(f32[8,256]{1,0:T(8,128)S(1)} %get-tuple-element.12.refs_0_), channel_id=1, source_target_pairs={{0,32},{2,34},{32,0},{34,2},{1,33},{3,35},{33,1},{35,3},{4,36},{6,... | collective-permute-start | bytes 24584 | tf_op jit(solution)/shard_map/ppermute | solution.py:262
  79.3 5.9 %collective-permute-start.6 = (f32[8,256]{1,0:T(8,128)S(1)}, f32[8,256]{1,0:T(8,128)S(1)}, u32[]{:S(2)}, u32[]{:S(2)}) collective-permute-start(f32[8,256]{1,0:T(8,128)S(1)} %get-tuple-element.12.refs_0_), channel_id=1, source_target_pairs={{0,2},{2,0},{32,34},{34,32},{1,3},{3,1},{33,35},{35,33},{4,6},{6,4... | collective-permute-start | bytes 24584 | tf_op jit(solution)/shard_map/ppermute | solution.py:262
  85.2 0.0 collective-permute-done.8.refs_3_
  85.2 0.0 collective-permute-done.7.refs_2_
  85.2 2.4 %collective-permute-done.6.refs_1_ = f32[8,256]{1,0:T(8,128)S(1)} collective-permute-done((f32[8,256]{1,0:T(8,128)S(1)}, f32[8,256]{1,0:T(8,128)S(1)}, u32[]{:S(2)}, u32[]{:S(2)}) %collective-permute-start.6) | collective-permute-done | bytes 8224 | tf_op jit(solution)/shard_map/ppermute | solution.py:262
  87.6 2.0 %collective-permute-start.11 = (f32[8,256]{1,0:T(8,128)S(1)}, f32[8,256]{1,0:T(8,128)S(1)}, u32[]{:S(2)}, u32[]{:S(2)}) collective-permute-start(f32[8,256]{1,0:T(8,128)S(1)} %merge.1.refs_0_), channel_id=1, source_target_pairs={{0,384},{128,256},{256,128},{384,0},{1,385},{129,257},{257,129},{3... | collective-permute-start | bytes 24584 | tf_op jit(solution)/shard_map/ppermute | solution.py:262
  89.6 4.4 %collective-permute-start.10 = (f32[8,256]{1,0:T(8,128)S(1)}, f32[8,256]{1,0:T(8,128)S(1)}, u32[]{:S(2)}, u32[]{:S(2)}) collective-permute-start(f32[8,256]{1,0:T(8,128)S(1)} %merge.1.refs_0_), channel_id=1, source_target_pairs={{0,256},{128,384},{256,0},{384,128},{1,257},{129,385},{257,1},{385... | collective-permute-start | bytes 24584 | tf_op jit(solution)/shard_map/ppermute | solution.py:262
  94.0 5.0 %collective-permute-start.9 = (f32[8,256]{1,0:T(8,128)S(1)}, f32[8,256]{1,0:T(8,128)S(1)}, u32[]{:S(2)}, u32[]{:S(2)}) collective-permute-start(f32[8,256]{1,0:T(8,128)S(1)} %merge.1.refs_0_), channel_id=1, source_target_pairs={{0,128},{128,0},{256,384},{384,256},{1,129},{129,1},{257,385},{385... | collective-permute-start | bytes 24584 | tf_op jit(solution)/shard_map/ppermute | solution.py:262
  99.0 0.0 collective-permute-done.11.refs_3_
  99.0 0.0 collective-permute-done.10.refs_2_
  99.0 1.4 collective-permute-done.9.refs_1_
  100.4 6.7 %grads.1 = bf16[32,160,128]{2,1,0:T(8,128)(2,1)S(1)} custom-call(bf16[32,128,128]{2,1,0:T(8,128)(2,1)S(1)} %all-to-all-done.in_ref, bf16[2048,128]{1,0:T(8,128)(2,1)S(1)} %fusion.1.mask_ref, bf16[2,16,64,128]{3,2,1,0:T(8,128)(2,1)S(1)} %get-tuple-element.11.qg_ref, f32[8,256]{1,0:T(8,128)S(1)} %merge.1.refs_0_, f32[8,256]{1,0:T(8,128)S(1)} %collective-permute-done.9.refs_1_, ...), custom_call_target="tpu_custom_call" | custom-call | flops 3221225472 | bytes 2097152 | tf_op jit(solution)/shard_map/grads/pallas_call | solution.py:302
  107.1 29.6 %all_to_all.24.back_ref = bf16[32,160,128]{2,1,0:T(8,128)(2,1)S(1)} all-to-all(bf16[32,160,128]{2,1,0:T(8,128)(2,1)S(1)} %grads.1), channel_id=1, replica_groups=mesh['zh'=4,'zl'=2,'ym'=2,'yl'=2,'x'=4,'yh'=2,'core'=2] {'zl','yl','x','..., dimensions={0} | all-to-all | bytes 2621440 | tf_op jit(solution)/shard_map/all_to_all | solution.py:312
  136.7 0.9 unpack_queries.1
  137.6 8.7 %all-to-all-start.3 = ((bf16[16,8,1024]{2,1,0:T(8,128)(2,1)}), bf16[16,8,1024]{2,1,0:T(8,128)(2,1)S(1)}, u32[]{:S(2)}, u32[]{:S(2)}) async-start(bf16[16,8,1024]{2,1,0:T(8,128)(2,1)} %bitcast.5), calls=%async_computation.3 | async-start | bytes 524288 | tf_op jit(solution)/shard_map/all_to_all | solution.py:314
  146.3 1.4 unpack_keys.1
  147.7 11.8 %all-to-all-done.3 = bf16[16,8,1024]{2,1,0:T(8,128)(2,1)S(1)} async-done(((bf16[16,8,1024]{2,1,0:T(8,128)(2,1)}), bf16[16,8,1024]{2,1,0:T(8,128)(2,1)S(1)}, u32[]{:S(2)}, u32[]{:S(2)}) %all-to-all-start.3) | async-done | bytes 262176 | tf_op jit(solution)/shard_map/all_to_all | solution.py:314
  159.6 0.6 reduce_sum.12
  (8 shorter events, 0.2 us)
Async XLA Ops:
  0.6 0.7 copy-start.4
  1.3 0.7 copy-start.5
  2.7 17.3 %all-to-all-start.1 = ((bf16[32,8,128]{2,1,0:T(8,128)(2,1)}), bf16[32,8,128]{2,1,0:T(8,128)(2,1)S(1)}, u32[]{:S(2)}, u32[]{:S(2)}) async-start(bf16[32,8,128]{2,1,0:T(8,128)(2,1)} %split.1), calls=%async_computation.1 | async-start | bytes 131072 | tf_op jit(solution)/shard_map/all_to_all | solution.py:277
  13.1 1.0 copy-start
  14.2 1.0 copy-start.1
  15.2 0.7 copy-start.2
  15.9 0.7 copy-start.3
  17.9 7.1 %copy-start.7 = (s32[2,32]{1,0:T(2,128)S(1)}, s32[2,32]{1,0:T(2,128)}, u32[]{:S(2)}) copy-start(s32[2,32]{1,0:T(2,128)} %param.14) | copy-start | bytes 772
  17.9 7.2 %copy-start.6 = (s32[2,248]{1,0:T(2,128)S(1)}, s32[2,248]{1,0:T(2,128)}, u32[]{:S(2)}) copy-start(s32[2,248]{1,0:T(2,128)} %param.15) | copy-start | bytes 5956
  20.0 50.0 %all-to-all-start = ((bf16[32,128,128]{2,1,0:T(8,128)(2,1)}), bf16[32,128,128]{2,1,0:T(8,128)(2,1)S(1)}, u32[]{:S(2)}, u32[]{:S(2)}) async-start(bf16[32,128,128]{2,1,0:T(8,128)(2,1)} %pack.1), calls=%async_computation | async-start | bytes 2097152 | tf_op jit(solution)/shard_map/all_to_all | solution.py:284
  25.3 14.7 %collective-permute-start.2 = (bf16[128,128]{1,0:T(8,128)(2,1)S(1)}, bf16[128,128]{1,0:T(8,128)(2,1)S(1)}, u32[]{:S(2)}, u32[]{:S(2)}) collective-permute-start(bf16[128,128]{1,0:T(8,128)(2,1)S(1)} %block.1), channel_id=1, source_target_pairs={{0,34},{2,32},{32,2},{34,0},{1,35},{3,33},{33,3},{35,1},{4,38},{6,... | collective-permute-start | bytes 98312 | tf_op jit(solution)/shard_map/ppermute | solution.py:262
  28.5 11.4 %collective-permute-start.1 = (bf16[128,128]{1,0:T(8,128)(2,1)S(1)}, bf16[128,128]{1,0:T(8,128)(2,1)S(1)}, u32[]{:S(2)}, u32[]{:S(2)}) collective-permute-start(bf16[128,128]{1,0:T(8,128)(2,1)S(1)} %block.1), channel_id=1, source_target_pairs={{0,32},{2,34},{32,0},{34,2},{1,33},{3,35},{33,1},{35,3},{4,36},{6,... | collective-permute-start | bytes 98312 | tf_op jit(solution)/shard_map/ppermute | solution.py:262
  32.3 10.0 %collective-permute-start = (bf16[128,128]{1,0:T(8,128)(2,1)S(1)}, bf16[128,128]{1,0:T(8,128)(2,1)S(1)}, u32[]{:S(2)}, u32[]{:S(2)}) collective-permute-start(bf16[128,128]{1,0:T(8,128)(2,1)S(1)} %block.1), channel_id=1, source_target_pairs={{0,2},{2,0},{32,34},{34,32},{1,3},{3,1},{33,35},{35,33},{4,6},{6,4... | collective-permute-start | bytes 98312 | tf_op jit(solution)/shard_map/ppermute | solution.py:262
  42.3 20.4 %collective-permute-start.5 = (bf16[4,128,128]{2,1,0:T(8,128)(2,1)S(1)}, bf16[4,128,128]{2,1,0:T(8,128)(2,1)S(1)}, u32[]{:S(2)}, u32[]{:S(2)}) collective-permute-start(bf16[4,128,128]{2,1,0:T(8,128)(2,1)S(1)} %pad_maximum_fusion.refs_0_), channel_id=1, source_target_pairs={{0,384},{128,256},{256,128},{384,0},{1,385},{129,257},{257,129},{3... | collective-permute-start | bytes 393224 | tf_op jit(solution)/shard_map/ppermute | solution.py:262
  52.0 15.0 %collective-permute-start.4 = (bf16[4,128,128]{2,1,0:T(8,128)(2,1)S(1)}, bf16[4,128,128]{2,1,0:T(8,128)(2,1)S(1)}, u32[]{:S(2)}, u32[]{:S(2)}) collective-permute-start(bf16[4,128,128]{2,1,0:T(8,128)(2,1)S(1)} %pad_maximum_fusion.refs_0_), channel_id=1, source_target_pairs={{0,256},{128,384},{256,0},{384,128},{1,257},{129,385},{257,1},{385... | collective-permute-start | bytes 393224 | tf_op jit(solution)/shard_map/ppermute | solution.py:262
  54.0 16.1 %collective-permute-start.3 = (bf16[4,128,128]{2,1,0:T(8,128)(2,1)S(1)}, bf16[4,128,128]{2,1,0:T(8,128)(2,1)S(1)}, u32[]{:S(2)}, u32[]{:S(2)}) collective-permute-start(bf16[4,128,128]{2,1,0:T(8,128)(2,1)S(1)} %pad_maximum_fusion.refs_0_), channel_id=1, source_target_pairs={{0,128},{128,0},{256,384},{384,256},{1,129},{129,1},{257,385},{385... | collective-permute-start | bytes 393224 | tf_op jit(solution)/shard_map/ppermute | solution.py:262
  73.8 11.4 %collective-permute-start.8 = (f32[8,256]{1,0:T(8,128)S(1)}, f32[8,256]{1,0:T(8,128)S(1)}, u32[]{:S(2)}, u32[]{:S(2)}) collective-permute-start(f32[8,256]{1,0:T(8,128)S(1)} %get-tuple-element.12.refs_0_), channel_id=1, source_target_pairs={{0,34},{2,32},{32,2},{34,0},{1,35},{3,33},{33,3},{35,1},{4,38},{6,... | collective-permute-start | bytes 24584 | tf_op jit(solution)/shard_map/ppermute | solution.py:262
  77.3 7.8 %collective-permute-start.7 = (f32[8,256]{1,0:T(8,128)S(1)}, f32[8,256]{1,0:T(8,128)S(1)}, u32[]{:S(2)}, u32[]{:S(2)}) collective-permute-start(f32[8,256]{1,0:T(8,128)S(1)} %get-tuple-element.12.refs_0_), channel_id=1, source_target_pairs={{0,32},{2,34},{32,0},{34,2},{1,33},{3,35},{33,1},{35,3},{4,36},{6,... | collective-permute-start | bytes 24584 | tf_op jit(solution)/shard_map/ppermute | solution.py:262
  79.3 8.3 %collective-permute-start.6 = (f32[8,256]{1,0:T(8,128)S(1)}, f32[8,256]{1,0:T(8,128)S(1)}, u32[]{:S(2)}, u32[]{:S(2)}) collective-permute-start(f32[8,256]{1,0:T(8,128)S(1)} %get-tuple-element.12.refs_0_), channel_id=1, source_target_pairs={{0,2},{2,0},{32,34},{34,32},{1,3},{3,1},{33,35},{35,33},{4,6},{6,4... | collective-permute-start | bytes 24584 | tf_op jit(solution)/shard_map/ppermute | solution.py:262
  87.6 11.4 %collective-permute-start.11 = (f32[8,256]{1,0:T(8,128)S(1)}, f32[8,256]{1,0:T(8,128)S(1)}, u32[]{:S(2)}, u32[]{:S(2)}) collective-permute-start(f32[8,256]{1,0:T(8,128)S(1)} %merge.1.refs_0_), channel_id=1, source_target_pairs={{0,384},{128,256},{256,128},{384,0},{1,385},{129,257},{257,129},{3... | collective-permute-start | bytes 24584 | tf_op jit(solution)/shard_map/ppermute | solution.py:262
  89.6 9.4 %collective-permute-start.10 = (f32[8,256]{1,0:T(8,128)S(1)}, f32[8,256]{1,0:T(8,128)S(1)}, u32[]{:S(2)}, u32[]{:S(2)}) collective-permute-start(f32[8,256]{1,0:T(8,128)S(1)} %merge.1.refs_0_), channel_id=1, source_target_pairs={{0,256},{128,384},{256,0},{384,128},{1,257},{129,385},{257,1},{385... | collective-permute-start | bytes 24584 | tf_op jit(solution)/shard_map/ppermute | solution.py:262
  94.0 6.4 %collective-permute-start.9 = (f32[8,256]{1,0:T(8,128)S(1)}, f32[8,256]{1,0:T(8,128)S(1)}, u32[]{:S(2)}, u32[]{:S(2)}) collective-permute-start(f32[8,256]{1,0:T(8,128)S(1)} %merge.1.refs_0_), channel_id=1, source_target_pairs={{0,128},{128,0},{256,384},{384,256},{1,129},{129,1},{257,385},{385... | collective-permute-start | bytes 24584 | tf_op jit(solution)/shard_map/ppermute | solution.py:262
  137.6 21.9 %all-to-all-start.3 = ((bf16[16,8,1024]{2,1,0:T(8,128)(2,1)}), bf16[16,8,1024]{2,1,0:T(8,128)(2,1)S(1)}, u32[]{:S(2)}, u32[]{:S(2)}) async-start(bf16[16,8,1024]{2,1,0:T(8,128)(2,1)} %bitcast.5), calls=%async_computation.3 | async-start | bytes 524288 | tf_op jit(solution)/shard_map/all_to_all | solution.py:314
